TPU v7x, 32 devices: a whole 2x2x4 slice. The times are simulated.
32 devices in a mesh: passage: 4 (over z), span: 8 (over y, x, core).
Axes of the slice: x: 2, y: 2, z: 4, core: 2. Of those that a mesh axis runs over, the one named last changes fastest.
Arguments:
- psi_rotor: float32 [6, 64, 64, 128], P(None, 'passage', 'span'), may hold values from -11 to 11
- psi_stator: float32 [6, 64, 64, 128], P(None, 'passage', 'span'), may hold values from -6 to 6
- rhs_rotor: float32 [6, 64, 64, 128], P(None, 'passage', 'span'), may hold values from -6 to 6
- rhs_stator: float32 [6, 64, 64, 128], P(None, 'passage', 'span'), may hold values from -6 to 6
- kappa_rotor: float32 [64, 64, 128], P('passage', 'span'), may hold values from 1 to 4
- kappa_stator: float32 [64, 64, 128], P('passage', 'span'), may hold values from 1 to 4
- rotor_blocks: float32 [7, 6, 6], replicated, may hold values from -0.5 to 1
- stator_blocks: float32 [7, 6, 6], replicated, may hold values from -0.5 to 1
- interface_block: float32 [6, 6], replicated, may hold values from -0.5 to 0.7
- pass_counts: int32 [4], P('passage'), may hold values from 8 to 16
- tile_source: int32 [8], replicated, may hold values from 0 to 7, as said below
Outputs:
- rotor_out: float32 [6, 64, 64, 128], P(None, 'passage', 'span')
- stator_out: float32 [6, 64, 64, 128], P(None, 'passage', 'span')
Inputs may be any that keep to these rules, and one draw needn't show every extreme that they name: `tile_source`: each stator span tile names one rotor span tile.
All inputs are finite; a program needn't handle non-finite values.
Results may differ from a plain program's by a relative error of at most 0.00011.
Values sent between devices are 32-bit elements; how exact they have to be, the bound alone decides.
A program may use at most 64 MiB of HBM per device.

v0:
```python
import jax
import jax.numpy as jnp
from jax import lax
from jax.sharding import PartitionSpec as P

ITERS = 3


def padded(shard, sides, width, wrap):
    for axis, dim in sides:
        size, length = (lax.axis_size(axis), shard.shape[dim])
        up = [(i, (i + 1) % size) for i in range(size if wrap else size - 1)]
        down = [(j, i) for i, j in up]
        last = lax.slice_in_dim(shard, length - width, length, axis=dim)
        first = lax.slice_in_dim(shard, 0, width, axis=dim)
        before = lax.ppermute(last, axis, up)
        after = lax.ppermute(first, axis, down)
        shard = jnp.concatenate([before, shard, after], axis=dim)
    return shard


def apply_block(block, field):
    return jnp.einsum("fg,gpsa->fpsa", block, field, precision=lax.Precision.HIGHEST)


def operator(field, pitch_ext, span_ext, kappa, blocks):
    cells_pitch = field.shape[1]
    cells_span = field.shape[2]
    pad_axial = jnp.pad(field, ((0, 0), (0, 0), (0, 0), (1, 1)))
    total = apply_block(blocks[1], pitch_ext[:, 0:cells_pitch])
    total = total + apply_block(blocks[2], pitch_ext[:, 2 : cells_pitch + 2])
    total = total + apply_block(blocks[3], span_ext[:, :, 0:cells_span])
    total = total + apply_block(blocks[4], span_ext[:, :, 2 : cells_span + 2])
    total = total + apply_block(blocks[5], pad_axial[:, :, :, :-2])
    total = total + apply_block(blocks[6], pad_axial[:, :, :, 2:])
    return kappa[None] * apply_block(blocks[0], field) - total


def outlet_mean(psi_rotor, pass_counts):
    cells_pitch = psi_rotor.shape[1]
    last = psi_rotor.shape[3] - 1
    mask = (jnp.arange(cells_pitch, dtype=jnp.int32) < pass_counts[0]).astype(jnp.float32)
    masked = psi_rotor[:, :, :, last] * mask[None, :, None]
    weight = jnp.sum(mask).reshape(1)
    rows_all, weights_all = (
        lax.all_gather(masked, "passage", axis=1, tiled=True),
        lax.all_gather(weight, "passage", axis=0, tiled=True),
    )
    total = jnp.sum(rows_all, axis=1)
    count = jnp.sum(weights_all)
    return total / count


def per_device(
    psi_rotor,
    psi_stator,
    rhs_rotor,
    rhs_stator,
    kappa_rotor,
    kappa_stator,
    rotor_blocks,
    stator_blocks,
    interface_block,
    pass_counts,
    tile_source,
):
    cells_span = psi_rotor.shape[2]
    band = lax.axis_index("span")
    source = tile_source[band]
    for step in range(ITERS):
        face_mean = outlet_mean(psi_rotor, pass_counts)
        profile = lax.all_gather(face_mean, "span", axis=1, tiled=True)
        inflow = lax.dynamic_slice_in_dim(profile, source * cells_span, cells_span, 1)
        inlet = jnp.dot(interface_block, inflow, precision=lax.Precision.HIGHEST)
        stacked = jnp.stack([psi_rotor, psi_stator])
        pitch_ext = padded(stacked, (("passage", 2),), 1, True)
        span_ext = padded(stacked, (("span", 3),), 1, False)
        res_rotor = rhs_rotor - operator(
            psi_rotor, pitch_ext[0], span_ext[0], kappa_rotor, rotor_blocks
        )
        res_stator = rhs_stator - operator(
            psi_stator, pitch_ext[1], span_ext[1], kappa_stator, stator_blocks
        )
        res_stator = res_stator.at[:, :, :, 0].add(inlet[:, None, :])
        psi_rotor = psi_rotor + 0.8 * res_rotor / kappa_rotor[None]
        psi_stator = psi_stator + 0.8 * res_stator / kappa_stator[None]
    return (psi_rotor, psi_stator)


def solution(mesh):
    return jax.shard_map(
        per_device,
        mesh=mesh,
        in_specs=(
            P(None, "passage", "span", None),
            P(None, "passage", "span", None),
            P(None, "passage", "span", None),
            P(None, "passage", "span", None),
            P("passage", "span", None),
            P("passage", "span", None),
            P(),
            P(),
            P(),
            P("passage"),
            P(),
        ),
        out_specs=(P(None, "passage", "span", None), P(None, "passage", "span", None)),
        check_vma=False,
    )
```

profile of v0, /device:TPU:0, one launch (start us, length us, event | category | flops | bytes accessed | tf_op | source)
XLA Modules:
  0.0 197.2 jit_solution(1249204586182248834)
XLA Ops:
  0.6 1.6 copy_bitcast_fusion
  2.9 3.0 %collective-permute-start = (f32[2,6,1,8,128]{4,1,3,2,0:T(8,128)}, f32[2,6,1,8,128]{4,1,3,2,0:T(8,128)}, u32[]{:S(2)}, u32[]{:S(2)}) collective-permute-start(f32[2,6,1,8,128]{4,1,3,2,0:T(8,128)} %get-tuple-element.56), channel_id=1, source_target_pairs={{0,8},{8,16},{16,24},{24,0},{1,9},{9,17},{17,25},{25,1},{2,10},{10... | collective-permute-start | bytes 147464 | tf_op jit(solution)/shard_map/ppermute | solution.py:16
  5.9 2.0 %collective-permute-start.1 = (f32[2,6,1,8,128]{4,1,3,2,0:T(8,128)}, f32[2,6,1,8,128]{4,1,3,2,0:T(8,128)}, u32[]{:S(2)}, u32[]{:S(2)}) collective-permute-start(f32[2,6,1,8,128]{4,1,3,2,0:T(8,128)} %get-tuple-element.57), channel_id=1, source_target_pairs={{8,0},{16,8},{24,16},{0,24},{9,1},{17,9},{25,17},{1,25},{10,2},{18... | collective-permute-start | bytes 147464 | tf_op jit(solution)/shard_map/ppermute | solution.py:17
  8.0 0.7 pad_maximum_fusion.11
  8.7 1.5 collective-permute-start.2
  10.1 1.3 collective-permute-start.3
  12.9 1.5 fusion.60
  17.7 1.4 dynamic-update-slice.9
  19.1 10.2 %all-reduce.6 = f32[4]{0:T(128)S(1)} all-reduce(f32[4]{0:T(128)S(1)} %dynamic-update-slice.9), channel_id=1, replica_groups=mesh['passage'=4,'span'=8] {'passage'}, use_global_device_ids=true, to_apply=%add.6 | all-reduce | flops 4 | bytes 32
  30.4 14.4 %all_gather.23 = f32[6,64,8]{2,0,1:T(8,128)S(1)} all-gather(f32[6,16,8]{2,0,1:T(8,128)S(1)} %copy.247), channel_id=1, replica_groups=mesh['passage'=4,'span'=8] {'passage'}, dimensions={1}, use_global_device_ids=true | all-gather | bytes 15360 | tf_op jit(solution)/shard_map/all_gather | solution.py:46
  44.9 0.7 broadcast_divide_fusion.2
  45.7 12.5 %all_gather.25 = f32[6,64]{0,1:T(8,128)S(1)} all-gather(f32[6,8]{0,1:T(8,128)S(1)} %copy.248), channel_id=1, replica_groups=mesh['passage'=4,'span'=8] {'span'}, dimensions={1}, use_global_device_ids=true | all-gather | bytes 1728 | tf_op jit(solution)/shard_map/all_gather | solution.py:72
  58.2 1.1 fusion.92
  59.4 1.5 fusion.57
  60.9 1.5 fusion.58
  62.3 1.6 convolution_multiply_fusion.3
  63.9 0.8 convolution_multiply_fusion.5
  64.9 1.0 pad_maximum_fusion.3
  68.3 1.1 pad_maximum_fusion
  70.0 1.2 fusion.24
  71.2 1.5 fusion.61
  72.7 1.5 fusion.62
  74.2 1.4 convolution_multiply_fusion.4
  76.1 0.9 fusion.26
  77.2 2.0 %scatter-add.10 = f32[6,16,8,128]{3,0,2,1:T(8,128)S(1)} dynamic-update-slice(f32[6,16,8,128]{3,0,2,1:T(8,128)S(1)} %fusion.26, f32[6,16,8,1]{3,0,2,1:T(8,128)S(1)} %slice_add_fusion.2, s32[]{:T(128)} %constant.78.clone.1, s32[]{:T(128)} %constant.78.clone.1, s32[]{:T(128)} %constant.78.clone.1, s32[]{:T(128)} %constant.78.clone.1) | dynamic-update-slice | bytes 6148 | tf_op jit(solution)/shard_map/scatter-add | solution.py:84
  79.5 1.4 convolution_multiply_fusion.1
  80.9 1.5 fusion.63
  82.4 1.5 fusion.64
  84.0 3.8 %collective-permute-start.5 = (f32[2,6,1,8,128]{4,1,3,2,0:T(8,128)S(1)}, f32[2,6,1,8,128]{4,1,3,2,0:T(8,128)S(1)}, u32[]{:S(2)}, u32[]{:S(2)}) collective-permute-start(f32[2,6,1,8,128]{4,1,3,2,0:T(8,128)S(1)} %get-tuple-element.53), channel_id=1, source_target_pairs={{8,0},{16,8},{24,16},{0,24},{9,1},{17,9},{25,17},{1,25},{10,2},{18... | collective-permute-start | bytes 147464 | tf_op jit(solution)/shard_map/ppermute | solution.py:17
  88.0 1.7 collective-permute-start.6
  89.7 1.3 collective-permute-start.7
  91.0 1.0 copy.253
  94.4 1.4 convolution_add_fusion.5
  95.8 1.0 pad_maximum_fusion.1
  97.5 1.4 fusion.48
  98.9 1.0 fusion.32
  99.9 1.0 slice.436
  100.9 1.4 copy.258
  102.4 15.2 %all_gather.26 = f32[6,64,8]{2,0,1:T(8,128)} all-gather(f32[6,16,8]{2,0,1:T(8,128)S(1)} %copy.254), channel_id=1, replica_groups=mesh['passage'=4,'span'=8] {'passage'}, dimensions={1}, use_global_device_ids=true | all-gather | bytes 15360 | tf_op jit(solution)/shard_map/all_gather | solution.py:46
  117.7 1.0 reduce_sum.49
  119.4 11.2 %all_gather.27 = f32[6,64]{0,1:T(8,128)S(1)} all-gather(f32[6,8]{0,1:T(8,128)S(1)} %copy.255), channel_id=1, replica_groups=mesh['passage'=4,'span'=8] {'span'}, dimensions={1}, use_global_device_ids=true | all-gather | bytes 1728 | tf_op jit(solution)/shard_map/all_gather | solution.py:72
  130.7 3.2 %fusion.35 = f32[6,16,8,128]{3,0,2,1:T(8,128)} fusion(f32[16,8,128,6]{2,3,1,0:T(8,128)} %convolution_multiply_fusion.1, f32[16,8,128,6]{2,3,1,0:T(8,128)} %fusion.64, f32[16,8,128,6]{2,3,1,0:T(8,128)} %fusion.63, f32[16,8,128,6]{2,3,1,0:T(8,128)} %fusion.48, f32[16,8,128,6]{2,3,1,0:T(8,128)S(1)} %copy-done.9, ...), kind=kOutput, calls=%fused_computation.68 | convolution fusion | flops 7667712 | bytes 3542016 | tf_op jit(solution)/shard_map/fg,gpsa->fpsa/dot_general | solution.py:23
  133.9 1.2 slice_add_fusion.1
  135.1 3.3 %scatter-add.11 = f32[6,16,8,128]{3,0,2,1:T(8,128)} dynamic-update-slice(f32[6,16,8,128]{3,0,2,1:T(8,128)} %fusion.35, f32[6,16,8,1]{3,0,2,1:T(8,128)S(1)} %slice_add_fusion.1, s32[]{:T(128)} %constant.78.clone.1, s32[]{:T(128)} %constant.78.clone.1, s32[]{:T(128)} %constant.78.clone.1, s32[]{:T(128)} %constant.78.clone.1) | dynamic-update-slice | bytes 6148 | tf_op jit(solution)/shard_map/scatter-add | solution.py:84
  138.4 1.2 divide_add_fusion.1
  140.2 1.4 convolution_multiply_fusion
  141.6 1.5 fusion.67
  143.1 1.5 fusion.68
  144.6 1.5 fusion.65
  146.1 1.5 fusion.66
  147.5 1.4 convolution_multiply_fusion.2
  148.9 3.8 %collective-permute-start.9 = (f32[2,6,1,8,128]{4,1,3,2,0:T(8,128)S(1)}, f32[2,6,1,8,128]{4,1,3,2,0:T(8,128)S(1)}, u32[]{:S(2)}, u32[]{:S(2)}) collective-permute-start(f32[2,6,1,8,128]{4,1,3,2,0:T(8,128)S(1)} %get-tuple-element.49), channel_id=1, source_target_pairs={{8,0},{16,8},{24,16},{0,24},{9,1},{17,9},{25,17},{1,25},{10,2},{18... | collective-permute-start | bytes 147464 | tf_op jit(solution)/shard_map/ppermute | solution.py:17
  152.7 1.7 collective-permute-start.10
  154.4 1.3 collective-permute-start.11
  155.8 14.4 %all_gather.28 = f32[6,64,8]{2,0,1:T(8,128)S(1)} all-gather(f32[6,16,8]{2,0,1:T(8,128)S(1)} %copy.259), channel_id=1, replica_groups=mesh['passage'=4,'span'=8] {'passage'}, dimensions={1}, use_global_device_ids=true | all-gather | bytes 15360 | tf_op jit(solution)/shard_map/all_gather | solution.py:46
  171.0 11.3 %all_gather.29 = f32[6,64]{0,1:T(8,128)S(1)} all-gather(f32[6,8]{0,1:T(8,128)S(1)} %copy.260), channel_id=1, replica_groups=mesh['passage'=4,'span'=8] {'span'}, dimensions={1}, use_global_device_ids=true | all-gather | bytes 1728 | tf_op jit(solution)/shard_map/all_gather | solution.py:72
  184.4 1.4 convolution_add_fusion.3
  186.5 1.4 fusion.49
  187.9 0.9 fusion.44
  188.8 0.9 slice_add_fusion
  189.7 2.4 %scatter-add.14 = f32[6,16,8,128]{3,0,2,1:T(8,128)S(1)} dynamic-update-slice(f32[6,16,8,128]{3,0,2,1:T(8,128)S(1)} %fusion.44, f32[6,16,8,1]{3,0,2,1:T(8,128)} %slice_add_fusion, s32[]{:T(128)} %constant.78.clone.1, s32[]{:T(128)} %constant.78.clone.1, s32[]{:T(128)} %constant.78.clone.1, s32[]{:T(128)} %constant.78.clone.1) | dynamic-update-slice | bytes 6148 | tf_op jit(solution)/shard_map/scatter-add | solution.py:84
  192.3 0.8 copy.262
  193.9 2.0 %fusion.41 = f32[6,16,8,128]{3,0,2,1:T(8,128)S(1)} fusion(f32[6,16,8,128]{3,0,2,1:T(8,128)S(1)} %fusion.32, f32[16,8,128,6]{2,3,1,0:T(8,128)S(1)} %copy-done.18, f32[16,8,128,6]{2,3,1,0:T(8,128)S(1)} %copy-done.17, f32[16,8,128,6]{2,3,1,0:T(8,128)S(1)} %copy-done.16, f32[16,8,128,6]{2,3,1,0:T(8,128)} %fusion.49, f32[16,8,128,6]{2,3,1,0:T(8,128)S(1)} %copy-done.15, ...), kind=kOutput, calls=%fused_computation.74 | convolution fusion | flops 7962624 | bytes 4525056 | tf_op jit(solution)/shard_map/fg,gpsa->fpsa/dot_general | solution.py:23
  195.9 0.8 copy.261
  (185 shorter events, 18.8 us)
Async XLA Ops:
  0.6 64.1 %copy-start = (f32[6,6]{1,0:T(8,128)S(1)}, f32[6,6]{1,0:T(8,128)}, u32[]{:S(2)}) copy-start(f32[6,6]{1,0:T(8,128)} %param.25) | copy-start | bytes 436
  2.2 9.2 %copy-start.1 = (f32[6,16,8,128]{3,2,1,0:T(8,128)S(1)}, f32[6,16,8,128]{3,2,1,0:T(8,128)}, u32[]{:S(2)}) copy-start(f32[6,16,8,128]{3,2,1,0:T(8,128)} %param.17) | copy-start | bytes 1179652
  2.9 8.7 %copy-start.55 = (f32[7,6,6]{2,0,1:T(8,128)S(1)}, f32[7,6,6]{2,0,1:T(8,128)}, u32[]{:S(2)}) copy-start(f32[7,6,6]{2,0,1:T(8,128)} %param.24) | copy-start | bytes 3028
  2.9 61.9 %collective-permute-start = (f32[2,6,1,8,128]{4,1,3,2,0:T(8,128)}, f32[2,6,1,8,128]{4,1,3,2,0:T(8,128)}, u32[]{:S(2)}, u32[]{:S(2)}) collective-permute-start(f32[2,6,1,8,128]{4,1,3,2,0:T(8,128)} %get-tuple-element.56), channel_id=1, source_target_pairs={{0,8},{8,16},{16,24},{24,0},{1,9},{9,17},{17,25},{25,1},{2,10},{10... | collective-permute-start | bytes 147464 | tf_op jit(solution)/shard_map/ppermute | solution.py:16
  5.9 58.9 %collective-permute-start.1 = (f32[2,6,1,8,128]{4,1,3,2,0:T(8,128)}, f32[2,6,1,8,128]{4,1,3,2,0:T(8,128)}, u32[]{:S(2)}, u32[]{:S(2)}) collective-permute-start(f32[2,6,1,8,128]{4,1,3,2,0:T(8,128)} %get-tuple-element.57), channel_id=1, source_target_pairs={{8,0},{16,8},{24,16},{0,24},{9,1},{17,9},{25,17},{1,25},{10,2},{18... | collective-permute-start | bytes 147464 | tf_op jit(solution)/shard_map/ppermute | solution.py:17
  8.7 59.6 %collective-permute-start.2 = (f32[2,6,16,1,128]{4,1,3,2,0:T(8,128)}, f32[2,6,16,1,128]{4,1,3,2,0:T(8,128)S(1)}, u32[]{:S(2)}, u32[]{:S(2)}) collective-permute-start(f32[2,6,16,1,128]{4,1,3,2,0:T(8,128)} %get-tuple-element.58), channel_id=1, source_target_pairs={{0,1},{1,2},{2,3},{3,4},{4,5},{5,6},{6,7},{8,9},{9,10},{10,11},{11... | collective-permute-start | bytes 294920 | tf_op jit(solution)/shard_map/ppermute | solution.py:16
  10.1 58.1 %collective-permute-start.3 = (f32[2,6,16,1,128]{4,1,3,2,0:T(8,128)S(1)}, f32[2,6,16,1,128]{4,1,3,2,0:T(8,128)}, u32[]{:S(2)}, u32[]{:S(2)}) collective-permute-start(f32[2,6,16,1,128]{4,1,3,2,0:T(8,128)S(1)} %get-tuple-element.59), channel_id=1, source_target_pairs={{1,0},{2,1},{3,2},{4,3},{5,4},{6,5},{7,6},{9,8},{10,9},{11,10},{12... | collective-permute-start | bytes 294920 | tf_op jit(solution)/shard_map/ppermute | solution.py:17
  11.4 3.0 %copy-start.58 = (s32[8]{0:T(128)S(1)}, s32[8]{0:T(128)}, u32[]{:S(2)}) copy-start(s32[8]{0:T(128)} %param.27) | copy-start | bytes 100
  11.4 5.6 %copy-start.59 = (u32[32]{0:T(128)S(1)}, u32[32]{0:T(128)}, u32[]{:S(2)}) copy-start(u32[32]{0:T(128)} %constant.98) | copy-start | bytes 388
  12.2 17.7 %copy-start.31 = (f32[1,6,6]{2,0,1:T(1,128)}, f32[1,6,6]{2,0,1:T(1,128)S(1)}, u32[]{:S(2)}) copy-start(f32[1,6,6]{2,0,1:T(1,128)S(1)} %get-tuple-element.70) | copy-start | bytes 436
  12.2 17.7 %copy-start.34 = (f32[1,6,6]{2,0,1:T(1,128)}, f32[1,6,6]{2,0,1:T(1,128)S(1)}, u32[]{:S(2)}) copy-start(f32[1,6,6]{2,0,1:T(1,128)S(1)} %get-tuple-element.65) | copy-start | bytes 436
  29.9 29.4 %copy-start.56 = (f32[16]{0:T(128)}, f32[16]{0:T(128)S(1)}, u32[]{:S(2)}) copy-start(f32[16]{0:T(128)S(1)} %compare_convert_fusion) | copy-start | bytes 196
  44.8 17.5 %copy-start.6 = (f32[6,16,8,128]{3,2,1,0:T(8,128)S(1)}, f32[6,16,8,128]{3,2,1,0:T(8,128)}, u32[]{:S(2)}) copy-start(f32[6,16,8,128]{3,2,1,0:T(8,128)} %param.18) | copy-start | bytes 1179652
  44.8 17.5 %copy-start.8 = (f32[16,8,128]{2,1,0:T(8,128)S(1)}, f32[16,8,128]{2,1,0:T(8,128)}, u32[]{:S(2)}) copy-start(f32[16,8,128]{2,1,0:T(8,128)} %param.22) | copy-start | bytes 196612
  44.9 17.4 %copy-start.37 = (f32[1,6,6]{2,0,1:T(1,128)S(1)}, f32[1,6,6]{2,0,1:T(1,128)}, u32[]{:S(2)}) copy-start(f32[1,6,6]{2,0,1:T(1,128)} %get-tuple-element.69) | copy-start | bytes 436
  59.3 4.6 %copy-start.46 = (f32[1,6,6]{2,0,1:T(1,128)}, f32[1,6,6]{2,0,1:T(1,128)S(1)}, u32[]{:S(2)}) copy-start(f32[1,6,6]{2,0,1:T(1,128)S(1)} %get-tuple-element.76) | copy-start | bytes 436
  59.3 7.2 %copy-start.43 = (f32[1,6,6]{2,0,1:T(1,128)}, f32[1,6,6]{2,0,1:T(1,128)S(1)}, u32[]{:S(2)}) copy-start(f32[1,6,6]{2,0,1:T(1,128)S(1)} %get-tuple-element.74) | copy-start | bytes 436
  59.3 8.3 %copy-start.40 = (f32[1,6,6]{2,0,1:T(1,128)}, f32[1,6,6]{2,0,1:T(1,128)S(1)}, u32[]{:S(2)}) copy-start(f32[1,6,6]{2,0,1:T(1,128)S(1)} %get-tuple-element.75) | copy-start | bytes 436
  59.3 10.1 %copy-start.28 = (f32[1,6,6]{2,0,1:T(1,128)}, f32[1,6,6]{2,0,1:T(1,128)S(1)}, u32[]{:S(2)}) copy-start(f32[1,6,6]{2,0,1:T(1,128)S(1)} %get-tuple-element.73) | copy-start | bytes 436
  59.3 10.6 %copy-start.53 = (f32[1,6,6]{2,0,1:T(1,128)}, f32[1,6,6]{2,0,1:T(1,128)S(1)}, u32[]{:S(2)}) copy-start(f32[1,6,6]{2,0,1:T(1,128)S(1)} %get-tuple-element.71) | copy-start | bytes 436
  59.3 11.8 %copy-start.51 = (f32[1,6,6]{2,0,1:T(1,128)}, f32[1,6,6]{2,0,1:T(1,128)S(1)}, u32[]{:S(2)}) copy-start(f32[1,6,6]{2,0,1:T(1,128)S(1)} %get-tuple-element.72) | copy-start | bytes 436
  59.4 13.3 %copy-start.49 = (f32[1,6,6]{2,0,1:T(1,128)}, f32[1,6,6]{2,0,1:T(1,128)S(1)}, u32[]{:S(2)}) copy-start(f32[1,6,6]{2,0,1:T(1,128)S(1)} %get-tuple-element.77) | copy-start | bytes 436
  60.9 3.1 %copy-start.7 = (f32[16,8,128]{2,1,0:T(8,128)S(1)}, f32[16,8,128]{2,1,0:T(8,128)}, u32[]{:S(2)}) copy-start(f32[16,8,128]{2,1,0:T(8,128)} %param.21) | copy-start | bytes 196612
  64.7 1.2 copy-start.25
  68.2 1.8 copy-start.3
  68.2 1.8 copy-start.22
  68.2 1.8 copy-start.23
  71.2 3.0 %copy-start.47 = (f32[1,6,6]{2,0,1:T(1,128)S(1)}, f32[1,6,6]{2,0,1:T(1,128)}, u32[]{:S(2)}) copy-start(f32[1,6,6]{2,0,1:T(1,128)} %copy-done.46) | copy-start | bytes 436
  74.2 1.9 copy-start.2
  74.2 2.0 copy-start.10
  74.2 2.0 copy-start.14
  77.2 2.4 %copy-start.38 = (f32[1,6,6]{2,0,1:T(1,128)S(1)}, f32[1,6,6]{2,0,1:T(1,128)}, u32[]{:S(2)}) copy-start(f32[1,6,6]{2,0,1:T(1,128)} %get-tuple-element.69) | copy-start | bytes 436
  79.2 1.7 copy-start.35
  79.5 2.9 %copy-start.32 = (f32[1,6,6]{2,0,1:T(1,128)S(1)}, f32[1,6,6]{2,0,1:T(1,128)}, u32[]{:S(2)}) copy-start(f32[1,6,6]{2,0,1:T(1,128)} %copy-done.31) | copy-start | bytes 436
  83.9 8.1 %collective-permute-start.4 = (f32[2,6,1,8,128]{4,1,3,2,0:T(8,128)S(1)}, f32[2,6,1,8,128]{4,1,3,2,0:T(8,128)S(1)}, u32[]{:S(2)}, u32[]{:S(2)}) collective-permute-start(f32[2,6,1,8,128]{4,1,3,2,0:T(8,128)S(1)} %get-tuple-element.52), channel_id=1, source_target_pairs={{0,8},{8,16},{16,24},{24,0},{1,9},{9,17},{17,25},{25,1},{2,10},{10... | collective-permute-start | bytes 147464 | tf_op jit(solution)/shard_map/ppermute | solution.py:16
  84.0 8.1 %collective-permute-start.5 = (f32[2,6,1,8,128]{4,1,3,2,0:T(8,128)S(1)}, f32[2,6,1,8,128]{4,1,3,2,0:T(8,128)S(1)}, u32[]{:S(2)}, u32[]{:S(2)}) collective-permute-start(f32[2,6,1,8,128]{4,1,3,2,0:T(8,128)S(1)} %get-tuple-element.53), channel_id=1, source_target_pairs={{8,0},{16,8},{24,16},{0,24},{9,1},{17,9},{25,17},{1,25},{10,2},{18... | collective-permute-start | bytes 147464 | tf_op jit(solution)/shard_map/ppermute | solution.py:17
  88.0 7.8 %collective-permute-start.6 = (f32[2,6,16,1,128]{4,1,3,2,0:T(8,128)S(1)}, f32[2,6,16,1,128]{4,1,3,2,0:T(8,128)S(1)}, u32[]{:S(2)}, u32[]{:S(2)}) collective-permute-start(f32[2,6,16,1,128]{4,1,3,2,0:T(8,128)S(1)} %get-tuple-element.54), channel_id=1, source_target_pairs={{0,1},{1,2},{2,3},{3,4},{4,5},{5,6},{6,7},{8,9},{9,10},{10,11},{11... | collective-permute-start | bytes 294920 | tf_op jit(solution)/shard_map/ppermute | solution.py:16
  89.7 6.1 %collective-permute-start.7 = (f32[2,6,16,1,128]{4,1,3,2,0:T(8,128)S(1)}, f32[2,6,16,1,128]{4,1,3,2,0:T(8,128)}, u32[]{:S(2)}, u32[]{:S(2)}) collective-permute-start(f32[2,6,16,1,128]{4,1,3,2,0:T(8,128)S(1)} %get-tuple-element.55), channel_id=1, source_target_pairs={{1,0},{2,1},{3,2},{4,3},{5,4},{6,5},{7,6},{9,8},{10,9},{11,10},{12... | collective-permute-start | bytes 294920 | tf_op jit(solution)/shard_map/ppermute | solution.py:17
  92.0 1.2 copy-start.26
  96.9 2.0 %copy-start.4 = (f32[6,16,8,128]{3,2,1,0:T(8,128)S(1)}, f32[6,16,8,128]{3,2,1,0:T(8,128)}, u32[]{:S(2)}) copy-start(f32[6,16,8,128]{3,2,1,0:T(8,128)} %param.19) | copy-start | bytes 1179652
  96.9 2.0 %copy-start.19 = (f32[16,8,128,6]{2,3,1,0:T(8,128)S(1)}, f32[16,8,128,6]{2,3,1,0:T(8,128)}, u32[]{:S(2)}) copy-start(f32[16,8,128,6]{2,3,1,0:T(8,128)} %fusion.61) | copy-start | bytes 1179652
  96.9 2.0 %copy-start.20 = (f32[16,8,128,6]{2,3,1,0:T(8,128)S(1)}, f32[16,8,128,6]{2,3,1,0:T(8,128)}, u32[]{:S(2)}) copy-start(f32[16,8,128,6]{2,3,1,0:T(8,128)} %fusion.62) | copy-start | bytes 1179652
  96.9 2.0 %copy-start.21 = (f32[16,8,128,6]{2,3,1,0:T(8,128)S(1)}, f32[16,8,128,6]{2,3,1,0:T(8,128)}, u32[]{:S(2)}) copy-start(f32[16,8,128,6]{2,3,1,0:T(8,128)} %convolution_multiply_fusion.4) | copy-start | bytes 1179652
  96.9 2.0 %copy-start.54 = (f32[1,6,6]{2,0,1:T(1,128)S(1)}, f32[1,6,6]{2,0,1:T(1,128)}, u32[]{:S(2)}) copy-start(f32[1,6,6]{2,0,1:T(1,128)} %copy-done.53) | copy-start | bytes 436
  99.9 2.4 %copy-start.24 = (f32[6,16,8,1]{1,2,3,0:T(8,128)S(1)}, f32[6,16,8,1]{1,2,3,0:T(8,128)}, u32[]{:S(2)}) copy-start(f32[6,16,8,1]{1,2,3,0:T(8,128)} %copy.253) | copy-start | bytes 9220
  99.9 2.4 %copy-start.57 = (f32[16]{0:T(128)S(1)}, f32[16]{0:T(128)}, u32[]{:S(2)}) copy-start(f32[16]{0:T(128)} %copy-done.56) | copy-start | bytes 196
  99.9 30.8 %copy-start.9 = (f32[16,8,128,6]{2,3,1,0:T(8,128)S(1)}, f32[16,8,128,6]{2,3,1,0:T(8,128)}, u32[]{:S(2)}) copy-start(f32[16,8,128,6]{2,3,1,0:T(8,128)} %convolution_add_fusion.5) | copy-start | bytes 1179652
  139.6 2.0 %copy-start.36 = (f32[1,6,6]{2,0,1:T(1,128)S(1)}, f32[1,6,6]{2,0,1:T(1,128)}, u32[]{:S(2)}) copy-start(f32[1,6,6]{2,0,1:T(1,128)} %copy-done.34) | copy-start | bytes 436
  140.2 2.9 %copy-start.33 = (f32[1,6,6]{2,0,1:T(1,128)S(1)}, f32[1,6,6]{2,0,1:T(1,128)}, u32[]{:S(2)}) copy-start(f32[1,6,6]{2,0,1:T(1,128)} %copy-done.31) | copy-start | bytes 436
  141.6 3.0 %copy-start.52 = (f32[1,6,6]{2,0,1:T(1,128)S(1)}, f32[1,6,6]{2,0,1:T(1,128)}, u32[]{:S(2)}) copy-start(f32[1,6,6]{2,0,1:T(1,128)} %copy-done.51) | copy-start | bytes 436
  143.1 3.0 %copy-start.50 = (f32[1,6,6]{2,0,1:T(1,128)S(1)}, f32[1,6,6]{2,0,1:T(1,128)}, u32[]{:S(2)}) copy-start(f32[1,6,6]{2,0,1:T(1,128)} %copy-done.49) | copy-start | bytes 436
  144.6 3.0 %copy-start.48 = (f32[1,6,6]{2,0,1:T(1,128)S(1)}, f32[1,6,6]{2,0,1:T(1,128)}, u32[]{:S(2)}) copy-start(f32[1,6,6]{2,0,1:T(1,128)} %copy-done.46) | copy-start | bytes 436
  148.9 33.5 %collective-permute-start.8 = (f32[2,6,1,8,128]{4,1,3,2,0:T(8,128)S(1)}, f32[2,6,1,8,128]{4,1,3,2,0:T(8,128)S(1)}, u32[]{:S(2)}, u32[]{:S(2)}) collective-permute-start(f32[2,6,1,8,128]{4,1,3,2,0:T(8,128)S(1)} %get-tuple-element.48), channel_id=1, source_target_pairs={{0,8},{8,16},{16,24},{24,0},{1,9},{9,17},{17,25},{25,1},{2,10},{10... | collective-permute-start | bytes 147464 | tf_op jit(solution)/shard_map/ppermute | solution.py:16
  148.9 33.6 %collective-permute-start.9 = (f32[2,6,1,8,128]{4,1,3,2,0:T(8,128)S(1)}, f32[2,6,1,8,128]{4,1,3,2,0:T(8,128)S(1)}, u32[]{:S(2)}, u32[]{:S(2)}) collective-permute-start(f32[2,6,1,8,128]{4,1,3,2,0:T(8,128)S(1)} %get-tuple-element.49), channel_id=1, source_target_pairs={{8,0},{16,8},{24,16},{0,24},{9,1},{17,9},{25,17},{1,25},{10,2},{18... | collective-permute-start | bytes 147464 | tf_op jit(solution)/shard_map/ppermute | solution.py:17
  152.7 33.0 %collective-permute-start.10 = (f32[2,6,16,1,128]{4,1,3,2,0:T(8,128)S(1)}, f32[2,6,16,1,128]{4,1,3,2,0:T(8,128)S(1)}, u32[]{:S(2)}, u32[]{:S(2)}) collective-permute-start(f32[2,6,16,1,128]{4,1,3,2,0:T(8,128)S(1)} %get-tuple-element.50), channel_id=1, source_target_pairs={{0,1},{1,2},{2,3},{3,4},{4,5},{5,6},{6,7},{8,9},{9,10},{10,11},{11... | collective-permute-start | bytes 294920 | tf_op jit(solution)/shard_map/ppermute | solution.py:16
  154.4 31.4 %collective-permute-start.11 = (f32[2,6,16,1,128]{4,1,3,2,0:T(8,128)S(1)}, f32[2,6,16,1,128]{4,1,3,2,0:T(8,128)S(1)}, u32[]{:S(2)}, u32[]{:S(2)}) collective-permute-start(f32[2,6,16,1,128]{4,1,3,2,0:T(8,128)S(1)} %get-tuple-element.51), channel_id=1, source_target_pairs={{1,0},{2,1},{3,2},{4,3},{5,4},{6,5},{7,6},{9,8},{10,9},{11,10},{12... | collective-permute-start | bytes 294920 | tf_op jit(solution)/shard_map/ppermute | solution.py:17
  170.2 12.4 %copy-start.27 = (f32[1,6,6]{2,0,1:T(1,128)S(1)}, f32[1,6,6]{2,0,1:T(1,128)}, u32[]{:S(2)}) copy-start(f32[1,6,6]{2,0,1:T(1,128)} %get-tuple-element.67) | copy-start | bytes 436
  185.9 2.0 %copy-start.11 = (f32[16,8,128,6]{2,3,1,0:T(8,128)S(1)}, f32[16,8,128,6]{2,3,1,0:T(8,128)}, u32[]{:S(2)}) copy-start(f32[16,8,128,6]{2,3,1,0:T(8,128)} %convolution_multiply_fusion) | copy-start | bytes 1179652
  185.9 2.0 copy-start.12
  185.9 2.0 copy-start.13
  192.1 1.2 copy-start.15
  192.1 1.4 copy-start.16
  192.2 1.6 copy-start.17
  192.2 1.7 copy-start.18
  (8 other events, 7.2 us)
where the time goes:
time: 201 us; the launch traced here: 197 us
  blocking collectives  89.2 us (44%)
  matrix products  47.8 us (24%)
  local copies, waits for them, and re-layouts  22.1 us (11%)
  starting transfers between devices  21.4 us (11%)
  other arithmetic  13.2 us (7%)
  between operations  3.45 us (2%)
    dot_general x42, matrix products, apply_block(): jnp.einsum('fg,gpsa->fpsa', block, field, precision=lax.Precision.HIGHEST)  47.4 us
    all_gather x3, blocking collectives, outlet_mean(): lax.all_gather(masked, 'passage', axis=1, tiled=True)  44.1 us
    all_gather x3, blocking collectives, per_device(): profile = lax.all_gather(face_mean, 'span', axis=1, tiled=True)  35 us
    ppermute x6, starting transfers between devices, padded(): after = lax.ppermute(first, axis, down)  13.5 us
    unnamed x1, blocking collectives  10.2 us
    ppermute x6, starting transfers between devices, padded(): before = lax.ppermute(last, axis, up)  7.87 us
    scatter-add x3, local copies, waits for them, and re-layouts, per_device(): res_stator = res_stator.at[:, :, :, 0].add(inlet[:, None, :])  7.69 us
    unnamed x126, local copies, waits for them, and re-layouts  6.15 us
  transfers between devices with their start and end apart: 12, of which 0 were waited for; matrix products, arithmetic and copies ran while one was open for 14% of the time, Pallas kernels for 0%

commit v1 on v0

v1 whole, which is shorter than its diff:
```python
import functools

import jax
import jax.numpy as jnp
from jax import lax
from jax.experimental import pallas as pl
from jax.experimental.pallas import tpu as pltpu
from jax.sharding import PartitionSpec as P

ITERS = 3
RELAX = 0.8
MESH = pl.DeviceIdType.MESH
F32 = jnp.float32
BF16 = jnp.bfloat16
ROTOR, STATOR = 0, 1


def split(x):
    hi = x.astype(BF16)
    lo = (x - hi.astype(F32)).astype(BF16)
    return hi, lo


def kernel(fields, cp, cs, ca, npass, nspan, *refs):
    it = iter(refs)

    def take(n):
        return [next(it) for _ in range(n)]

    psi_in = take(2)
    rhs_in = take(2)
    kap_in = take(2)
    blocks = take(2)
    (iface, counts, source) = take(3)
    outs = take(2)
    psi = [take(ITERS + 1) for _ in range(2)]
    rhs = take(2)
    coef = take(2)
    cen = [[take(2) for _ in range(ITERS)] for _ in range(2)]
    ext = [[take(2) for _ in range(ITERS)] for _ in range(2)]
    mat = take(2)
    (psend, precv, ssend, srecv, fsend, frecv, msend) = take(7)
    mrecv = take(ITERS)
    (in_sem, out_sem, hs_sem, hr_sem, fs_sem, fr_sem, ms_sem, mr_sem) = take(8)

    nb = fields * cs
    kx = 2 * nb + 16
    plane = cp * cs

    ip = lax.axis_index("passage")
    js = lax.axis_index("span")
    right = lax.rem(ip + 1, npass)
    left = lax.rem(ip + npass - 1, npass)

    loads = {}
    for n, (src, dst, name) in enumerate(
        [
            (psi_in[0], psi[0][0], "psi0"),
            (psi_in[1], psi[1][0], "psi1"),
            (kap_in[0], coef[0], "kap0"),
            (rhs_in[0], rhs[0], "rhs0"),
            (kap_in[1], coef[1], "kap1"),
            (rhs_in[1], rhs[1], "rhs1"),
        ]
    ):
        loads[name] = pltpu.make_async_copy(src, dst, in_sem.at[n])
        loads[name].start()

    srecv[...] = jnp.zeros_like(srecv)

    barrier = pltpu.get_barrier_semaphore()
    for o in range(1, npass):
        pl.semaphore_signal(
            barrier, inc=1, device_id=(lax.rem(ip + o, npass), js), device_id_type=MESH
        )
    for o in range(1, nspan):
        pl.semaphore_signal(
            barrier, inc=1, device_id=(ip, lax.rem(js + o, nspan)), device_id_type=MESH
        )

    def halo_copies(r, k):
        made = []
        for d, target in ((0, (right, js)), (1, (left, js))):
            made.append(
                pltpu.make_async_remote_copy(
                    src_ref=psend.at[r, k, d],
                    dst_ref=precv.at[r, k, d],
                    send_sem=hs_sem.at[r, k, d],
                    recv_sem=hr_sem.at[r, k, d],
                    device_id=target,
                    device_id_type=MESH,
                )
            )
        for d, target in (
            (0, (ip, lax.rem(js + 1, nspan))),
            (1, (ip, lax.rem(js + nspan - 1, nspan))),
        ):
            made.append(
                pltpu.make_async_remote_copy(
                    src_ref=ssend.at[r, k, d],
                    dst_ref=srecv.at[r, k, d, pl.ds(0, fields * cp)],
                    send_sem=hs_sem.at[r, k, 2 + d],
                    recv_sem=hr_sem.at[r, k, 2 + d],
                    device_id=target,
                    device_id_type=MESH,
                )
            )
        return made

    halos = {(r, k): halo_copies(r, k) for r in range(2) for k in range(ITERS)}
    has_next, has_prev = js < nspan - 1, js > 0

    def send_halos(r, k):
        for d, p in ((0, cp - 1), (1, 0)):
            for f in range(fields):
                psend[r, k, d, pl.ds(f * cs, cs), :] = psi[r][k][
                    pl.ds(f * plane + p * cs, cs), :
                ]
        for d, s in ((0, cs - 1), (1, 0)):
            for f in range(fields):
                ssend[r, k, d, pl.ds(f * cp, cp), :] = psi[r][k][
                    pl.ds(f * plane + s, cp, stride=cs), :
                ]
        to_right, to_left, to_next, to_prev = halos[r, k]

        @pl.when(has_next)
        def _():
            to_next.start()

        @pl.when(has_prev)
        def _():
            to_prev.start()

        to_right.start()
        to_left.start()

    def finish_sends(r, k):
        to_right, to_left, to_next, to_prev = halos[r, k]
        to_right.wait_send()
        to_left.wait_send()

        @pl.when(has_next)
        def _():
            to_next.wait_send()

        @pl.when(has_prev)
        def _():
            to_prev.wait_send()

    def receive_halos(r, k):
        to_right, to_left, to_next, to_prev = halos[r, k]
        to_right.wait_recv()
        to_left.wait_recv()

        @pl.when(has_prev)
        def _():
            to_next.wait_recv()

        @pl.when(has_next)
        def _():
            to_prev.wait_recv()

        chi, clo = cen[r][k]
        for d, p in ((0, 0), (1, cp + 1)):
            hi, lo = split(precv[r, k, d])
            chi[pl.ds(p * nb, nb), :] = hi
            clo[pl.ds(p * nb, nb), :] = lo
        xhi, xlo = ext[r][k]
        for p in range(cp):
            rows = [srecv[r, k, d, pl.ds(p, 8, stride=cp), :] for d in range(2)]
            hi, lo = split(jnp.concatenate(rows, axis=0))
            xhi[pl.ds(p * kx + 2 * nb, 16), :] = hi
            xlo[pl.ds(p * kx + 2 * nb, 16), :] = lo

    lane = lax.broadcasted_iota(jnp.int32, (cs, ca), 1)
    wide = lax.broadcasted_iota(jnp.int32, (nb, ca), 1)

    def face_copies(k):
        return [
            pltpu.make_async_remote_copy(
                src_ref=fsend.at[k],
                dst_ref=frecv.at[k, o],
                send_sem=fs_sem.at[k, o],
                recv_sem=fr_sem.at[k, o],
                device_id=(lax.rem(ip + o, npass), js),
                device_id_type=MESH,
            )
            for o in range(1, npass)
        ]

    def mean_copies(k):
        return [
            pltpu.make_async_remote_copy(
                src_ref=msend.at[k],
                dst_ref=mrecv[k].at[js],
                send_sem=ms_sem.at[k, o],
                recv_sem=mr_sem.at[k, o],
                device_id=(ip, lax.rem(js + o, nspan)),
                device_id_type=MESH,
            )
            for o in range(1, nspan)
        ]

    faces = [face_copies(k) for k in range(ITERS)]
    means = [mean_copies(k) for k in range(ITERS)]
    count = counts[0]

    def send_face(k):
        state = psi[ROTOR][k]
        tile = jnp.where(lane == fields, jnp.clip(count, 0, cp).astype(F32), 0.0)
        for f in range(fields):
            acc = jnp.zeros((cs, ca), F32)
            for p in range(cp):
                w = jnp.where(p < count, 1.0, 0.0).astype(F32)
                acc = acc + w * state[pl.ds(f * plane + p * cs, cs), :]
            tile = jnp.where(lane == f, pltpu.roll(acc, f + 1, 1), tile)
        fsend[k] = tile
        for c in faces[k]:
            c.start()

    def send_mean(k):
        total = fsend[k]
        for o, c in enumerate(faces[k]):
            c.wait_recv()
            total = total + frecv[k, o + 1]
        mean = total / total[:, fields : fields + 1]
        msend[k] = mean
        mrecv[k][js] = mean
        for c in means[k]:
            c.start()

    def inlet_rows(k):
        for c in means[k]:
            c.wait_recv()
        tile = mrecv[k][source[js]]
        moved = [
            jnp.where(lane == 0, pltpu.roll(tile, (ca - g) % ca, 1), 0.0) for g in range(fields)
        ]
        rows = []
        for f in range(fields):
            acc = iface[f, 0] * moved[0]
            for g in range(1, fields):
                acc = acc + iface[f, g] * moved[g]
            rows.append(acc)
        return jnp.concatenate(rows, axis=0)

    def build_matrix(r):
        kk = 5 * nb + 16
        col = lax.broadcasted_iota(jnp.int32, (cs, kk), 1)
        row = lax.broadcasted_iota(jnp.int32, (cs, kk), 0)
        part = col // nb
        g_in = (col - part * nb) // cs
        s_in = col - part * nb - g_in * cs
        tail = part == 5
        up = tail & (g_in == 0)
        down = tail & (g_in == 1)
        which = jnp.full((cs, kk), -1, jnp.int32)
        same = s_in == row
        which = jnp.where((part == 0) & same, 1, which)
        which = jnp.where((part == 2) & same, 2, which)
        which = jnp.where((part == 3) & same, 5, which)
        which = jnp.where((part == 4) & same, 6, which)
        which = jnp.where((part == 1) & (s_in + 1 == row), 3, which)
        which = jnp.where((part == 1) & (s_in == row + 1), 4, which)
        which = jnp.where(up & (row == 0), 3, which)
        which = jnp.where(down & (row == cs - 1), 4, which)
        field = jnp.where(tail, s_in, g_in)
        code = jnp.where(which >= 0, which * 8 + field, -1)
        middle = jnp.where((part == 1) & same, g_in, -1)
        near, main = [], []
        masks = [[code == (b * 8 + g) for g in range(fields)] for b in range(1, 7)]
        centre = [middle == g for g in range(fields)]
        for f in range(fields):
            acc = jnp.zeros((cs, kk), F32)
            mid = jnp.zeros((cs, kk), F32)
            for g in range(fields):
                mid = jnp.where(centre[g], -RELAX * blocks[r][0, f, g], mid)
                for b in range(1, 7):
                    acc = jnp.where(masks[b - 1][g], blocks[r][b, f, g], acc)
            near.append(acc)
            main.append(mid)
        hi, lo = split(jnp.concatenate(near + main, axis=0))
        mat[r][pl.ds(0, 2 * nb), :] = hi
        mat[r][pl.ds(2 * nb, 2 * nb), :] = lo

    def store_split(r, k, p, new):
        chi, clo = cen[r][k]
        xhi, xlo = ext[r][k]
        hi, lo = split(new)
        at = pl.ds(pl.multiple_of((p + 1) * nb, 16), nb)
        chi[at, :] = hi
        clo[at, :] = lo
        before = jnp.where(wide == 0, 0.0, pltpu.roll(new, 1, 1))
        after = jnp.where(wide == ca - 1, 0.0, pltpu.roll(new, ca - 1, 1))
        for n, value in enumerate((before, after)):
            hi, lo = split(value)
            at = pl.ds(pl.multiple_of(p * kx + n * nb, 16), nb)
            xhi[at, :] = hi
            xlo[at, :] = lo

    def cell(ref, p):
        return jnp.concatenate(
            [ref[pl.ds(pl.multiple_of(f * plane + p * cs, 8), cs), :] for f in range(fields)],
            axis=0,
        )

    def columns(c, x, p):
        return jnp.concatenate(
            [
                c[pl.ds(pl.multiple_of(p * nb, 16), 3 * nb), :],
                x[pl.ds(pl.multiple_of(p * kx, 16), kx), :],
            ],
            axis=0,
        )

    def advance(r, k, inlet):
        chi, clo = cen[r][k]
        xhi, xlo = ext[r][k]

        def pair(q):
            cells = (2 * q, 2 * q + 1)
            hi = jnp.concatenate([columns(chi, xhi, p) for p in cells], axis=1)
            lo = jnp.concatenate([columns(clo, xlo, p) for p in cells], axis=1)
            first = jnp.dot(mat[r][...], hi, preferred_element_type=F32)
            second = jnp.dot(mat[r][pl.ds(0, 2 * nb), :], lo, preferred_element_type=F32)
            both = first[: 2 * nb] + (first[2 * nb :] + second)
            for n, p in enumerate(cells):
                mine = both[:, n * ca : (n + 1) * ca]
                res = cell(rhs[r], p) + mine[:nb]
                if inlet is not None:
                    res = res + inlet
                c = coef[r][pl.ds(pl.multiple_of(p * cs, 8), cs), :]
                c = jnp.concatenate([c] * fields, axis=0)
                new = (cell(psi[r][k], p) + mine[nb:]) + c * res
                for f in range(fields):
                    psi[r][k + 1][pl.ds(pl.multiple_of(f * plane + p * cs, 8), cs), :] = new[
                        f * cs : (f + 1) * cs
                    ]
                if k + 1 < ITERS:
                    store_split(r, k + 1, p, new)

        pl.loop(0, cp // 2)(pair)

    pl.semaphore_wait(barrier, npass + nspan - 2)
    loads["psi0"].wait()
    send_halos(ROTOR, 0)
    send_face(0)
    loads["psi1"].wait()
    send_halos(STATOR, 0)

    for r in range(2):
        build_matrix(r)
        pl.loop(0, cp)(lambda p, r=r: store_split(r, 0, p, cell(psi[r][0], p)))
    for r in range(2):
        loads["kap%d" % r].wait()
        coef[r][...] = RELAX / coef[r][...]
        loads["rhs%d" % r].wait()

    stores = []
    for k in range(ITERS):
        send_mean(k)
        receive_halos(ROTOR, k)
        advance(ROTOR, k, None)
        if k + 1 < ITERS:
            send_halos(ROTOR, k + 1)
            send_face(k + 1)
        else:
            stores.append(pltpu.make_async_copy(psi[ROTOR][ITERS], outs[ROTOR], out_sem.at[0]))
            stores[-1].start()
        inlet = inlet_rows(k)
        receive_halos(STATOR, k)
        advance(STATOR, k, inlet)
        if k + 1 < ITERS:
            send_halos(STATOR, k + 1)
    stores.append(pltpu.make_async_copy(psi[STATOR][ITERS], outs[STATOR], out_sem.at[1]))
    stores[-1].start()
    for k in range(ITERS):
        for r in range(2):
            finish_sends(r, k)
        for c in faces[k] + means[k]:
            c.wait_send()
    for c in stores:
        c.wait()


def per_device(
    npass,
    nspan,
    psi_rotor,
    psi_stator,
    rhs_rotor,
    rhs_stator,
    kappa_rotor,
    kappa_stator,
    rotor_blocks,
    stator_blocks,
    interface_block,
    pass_counts,
    tile_source,
):
    fields, cp, cs, ca = psi_rotor.shape
    rows = fields * cp * cs
    flat = [x.reshape(rows, ca) for x in (psi_rotor, psi_stator, rhs_rotor, rhs_stator)]
    kaps = [x.reshape(cp * cs, ca) for x in (kappa_rotor, kappa_stator)]
    nb = fields * cs
    kx = 2 * nb + 16
    state = pltpu.VMEM((rows, ca), F32)
    scratch = [state] * (2 * (ITERS + 1))
    scratch += [state] * 2
    scratch += [pltpu.VMEM((cp * cs, ca), F32)] * 2
    scratch += [pltpu.VMEM(((cp + 2) * nb, ca), BF16)] * (2 * ITERS * 2)
    scratch += [pltpu.VMEM((cp * kx, ca), BF16)] * (2 * ITERS * 2)
    scratch += [pltpu.VMEM((4 * nb, 5 * nb + 16), BF16)] * 2
    scratch += [
        pltpu.VMEM((2, ITERS, 2, nb, ca), F32),
        pltpu.VMEM((2, ITERS, 2, nb, ca), F32),
        pltpu.VMEM((2, ITERS, 2, fields * cp, ca), F32),
        pltpu.VMEM((2, ITERS, 2, 8 * cp, ca), F32),
        pltpu.VMEM((ITERS, cs, ca), F32),
        pltpu.VMEM((ITERS, npass, cs, ca), F32),
        pltpu.VMEM((ITERS, cs, ca), F32),
    ]
    scratch += [pltpu.VMEM((nspan, cs, ca), F32)] * ITERS
    dma = pltpu.SemaphoreType.DMA
    scratch += [
        dma((6,)),
        dma((2,)),
        dma((2, ITERS, 4)),
        dma((2, ITERS, 4)),
        dma((ITERS, npass)),
        dma((ITERS, npass)),
        dma((ITERS, nspan)),
        dma((ITERS, nspan)),
    ]
    anywhere = pl.BlockSpec(memory_space=pltpu.HBM)
    smem = pl.BlockSpec(memory_space=pltpu.SMEM)
    out = pl.pallas_call(
        functools.partial(kernel, fields, cp, cs, ca, npass, nspan),
        out_shape=[jax.ShapeDtypeStruct((rows, ca), F32)] * 2,
        in_specs=[anywhere] * 6 + [smem] * 5,
        out_specs=[anywhere] * 2,
        scratch_shapes=scratch,
        compiler_params=pltpu.CompilerParams(
            collective_id=0, has_side_effects=True, vmem_limit_bytes=40 * 1024 * 1024
        ),
    )(*flat, *kaps, rotor_blocks, stator_blocks, interface_block, pass_counts, tile_source)
    return tuple(x.reshape(psi_rotor.shape) for x in out)


def solution(mesh):
    return jax.shard_map(
        functools.partial(per_device, mesh.shape["passage"], mesh.shape["span"]),
        mesh=mesh,
        in_specs=(
            P(None, "passage", "span", None),
            P(None, "passage", "span", None),
            P(None, "passage", "span", None),
            P(None, "passage", "span", None),
            P("passage", "span", None),
            P("passage", "span", None),
            P(),
            P(),
            P(),
            P("passage"),
            P(),
        ),
        out_specs=(P(None, "passage", "span", None), P(None, "passage", "span", None)),
        check_vma=False,
    )
```

time: 201 us -> 41.4 us (0.21); the launches traced: 197 us -> 40.9 us
  blocking collectives: 89.2 us -> 0 us
  matrix products: 47.8 us -> 0 us
  Pallas kernels: 0 us -> 31.7 us
  starting transfers between devices: 21.4 us -> 0 us
  local copies, waits for them, and re-layouts: 22.1 us -> 7.83 us
  other arithmetic: 13.2 us -> 0 us
  between operations: 3.45 us -> 1.36 us
    all_gather x6 -> x0, blocking collectives: 79 us -> none  [the longest x3 44.1 us: outlet_mean(): lax.all_gather(masked, 'passage', axis=1, tiled=True)]
    dot_general x45 -> x0, matrix products: 47.8 us -> none  [the longest x42 47.4 us: apply_block(): jnp.einsum('fg,gpsa->fpsa', block, field, precision=lax.Precision.HIGHEST)]
    pallas_call x0 -> x1, Pallas kernels: none -> 31.7 us  [per_device(): pl.pallas_call(functools.partial(kernel, fields, cp, cs, ca, npass, nspan...]
    ppermute x12 -> x0, starting transfers between devices: 21.4 us -> none  [the longest x6 13.5 us: padded(): after = lax.ppermute(first, axis, down)]
    unnamed x1 -> x0, blocking collectives: 10.2 us -> none
    scatter-add x3 -> x0, local copies, waits for them, and re-layouts: 7.69 us -> none  [per_device(): res_stator = res_stator.at[:, :, :, 0].add(inlet[:, None, :])]
    slice x7 -> x0, local copies, waits for them, and re-layouts: 5.49 us -> none  [the longest x5 3.77 us: outlet_mean(): masked = psi_rotor[:, :, :, last] * mask[None, :, None]]
    add x6 -> x0, other arithmetic: 3.8 us -> none  [the longest x3 2.21 us: per_device(): res_stator = res_stator.at[:, :, :, 0].add(inlet[:, None, :])]
  transfers between devices with their start and end apart: 12 -> 0, of which waited for: 0 -> 0; matrix products, arithmetic and copies ran while one was open for 14% -> 0% of each run, Pallas kernels for 0% -> 0%
where the time goes in v1:
time: 41.4 us; the launch traced here: 40.9 us
  Pallas kernels  31.7 us (77%)
  local copies, waits for them, and re-layouts  7.83 us (19%)
  between operations  1.36 us (3%)
    pallas_call x1, Pallas kernels, per_device(): pl.pallas_call(functools.partial(kernel, fields, cp, cs, ca, npass, nspan...  31.7 us
    unnamed x20, local copies, waits for them, and re-layouts  7.83 us

profile of v1, /device:TPU:0, one launch (start us, length us, event | category | flops | bytes accessed | tf_op | source)
XLA Modules:
  0.0 40.9 jit_solution(5803176097522236085)
XLA Ops:
  0.6 0.0 copy-start.4
  1.3 0.7 %copy.13.refs_6_ = f32[7,6,6]{2,1,0:T(8,128)S(1)} copy(f32[7,6,6]{2,0,1:T(8,128)} %param.17) | data formatting | bytes 2016 | tf_op args[6]
  2.1 0.0 copy-start.6
  2.1 0.0 copy-start.7
  2.1 0.8 %copy.14.refs_7_ = f32[7,6,6]{2,1,0:T(8,128)S(1)} copy(f32[7,6,6]{2,0,1:T(8,128)} %param.18) | data formatting | bytes 2016 | tf_op args[7]
  2.8 0.0 copy-done.4
  2.8 0.0 copy-done.6
  2.9 0.0 copy-done.7
  2.9 0.0 copy-start
  2.9 1.0 %copy-done = f32[6,16,8,128]{3,2,1,0:T(8,128)S(1)} copy-done((f32[6,16,8,128]{3,2,1,0:T(8,128)S(1)}, f32[6,16,8,128]{3,2,1,0:T(8,128)}, u32[]{:S(2)}) %copy-start) | copy-done | bytes 393240
  3.9 0.0 copy-start.1
  3.9 1.0 %copy-done.1 = f32[6,16,8,128]{3,2,1,0:T(8,128)S(1)} copy-done((f32[6,16,8,128]{3,2,1,0:T(8,128)S(1)}, f32[6,16,8,128]{3,2,1,0:T(8,128)}, u32[]{:S(2)}) %copy-start.1) | copy-done | bytes 393240
  4.9 0.0 copy-start.2
  4.9 1.0 %copy-done.2 = f32[6,16,8,128]{3,2,1,0:T(8,128)S(1)} copy-done((f32[6,16,8,128]{3,2,1,0:T(8,128)S(1)}, f32[6,16,8,128]{3,2,1,0:T(8,128)}, u32[]{:S(2)}) %copy-start.2) | copy-done | bytes 393240
  5.9 0.0 copy-start.3
  5.9 1.0 %copy-done.3 = f32[6,16,8,128]{3,2,1,0:T(8,128)S(1)} copy-done((f32[6,16,8,128]{3,2,1,0:T(8,128)S(1)}, f32[6,16,8,128]{3,2,1,0:T(8,128)}, u32[]{:S(2)}) %copy-start.3) | copy-done | bytes 393240
  6.9 0.0 copy-start.5
  6.9 0.8 %copy-done.5 = f32[16,8,128]{2,1,0:T(8,128)S(1)} copy-done((f32[16,8,128]{2,1,0:T(8,128)S(1)}, f32[16,8,128]{2,1,0:T(8,128)}, u32[]{:S(2)}) %copy-start.5) | copy-done | bytes 65560
  7.7 31.7 %shard_map.122 = (f32[768,128]{1,0:T(8,128)S(1)}, f32[768,128]{1,0:T(8,128)S(1)}) custom-call(f32[768,128]{1,0:T(8,128)S(1)} %bitcast.10, f32[768,128]{1,0:T(8,128)S(1)} %bitcast.11, f32[768,128]{1,0:T(8,128)S(1)} %bitcast.12, f32[768,128]{1,0:T(8,128)S(1)} %bitcast.13, f32[128,128]{1,0:T(8,128)S(1)} %bitcast.14, f32[128,128]{1,0:T(8,128)S(1)} %bitcast.15, ...), custom_call_target="tpu_custom_call" | custom-call | tf_op jit(solution)/shard_map/pallas_call | solution.py:437
  39.4 0.7 %copy.18 = f32[6,16,8,128]{3,2,1,0:T(8,128)} copy(f32[6,16,8,128]{3,2,1,0:T(8,128)S(1)} %bitcast.9) | data formatting | bytes 786432
  40.2 0.7 %copy.19 = f32[6,16,8,128]{3,2,1,0:T(8,128)} copy(f32[6,16,8,128]{3,2,1,0:T(8,128)S(1)} %bitcast.8) | data formatting | bytes 786432
Async XLA Ops:
  0.6 2.2 %copy-start.4 = (f32[16,8,128]{2,1,0:T(8,128)S(1)}, f32[16,8,128]{2,1,0:T(8,128)}, u32[]{:S(2)}) copy-start(f32[16,8,128]{2,1,0:T(8,128)} %param.15) | copy-start | bytes 196612
  2.1 0.8 %copy-start.6 = (f32[6,6]{1,0:T(8,128)S(1)}, f32[6,6]{1,0:T(8,128)}, u32[]{:S(2)}) copy-start(f32[6,6]{1,0:T(8,128)} %refs_8_.1) | copy-start | bytes 436
  2.1 0.8 %copy-start.7 = (s32[8]{0:T(128)S(1)}, s32[8]{0:T(128)}, u32[]{:S(2)}) copy-start(s32[8]{0:T(128)} %refs_10_.1) | copy-start | bytes 100
  2.9 1.0 %copy-start = (f32[6,16,8,128]{3,2,1,0:T(8,128)S(1)}, f32[6,16,8,128]{3,2,1,0:T(8,128)}, u32[]{:S(2)}) copy-start(f32[6,16,8,128]{3,2,1,0:T(8,128)} %param.11) | copy-start | bytes 1179652
  3.9 1.0 %copy-start.1 = (f32[6,16,8,128]{3,2,1,0:T(8,128)S(1)}, f32[6,16,8,128]{3,2,1,0:T(8,128)}, u32[]{:S(2)}) copy-start(f32[6,16,8,128]{3,2,1,0:T(8,128)} %param.12) | copy-start | bytes 1179652
  4.9 1.0 %copy-start.2 = (f32[6,16,8,128]{3,2,1,0:T(8,128)S(1)}, f32[6,16,8,128]{3,2,1,0:T(8,128)}, u32[]{:S(2)}) copy-start(f32[6,16,8,128]{3,2,1,0:T(8,128)} %param.13) | copy-start | bytes 1179652
  5.9 1.0 %copy-start.3 = (f32[6,16,8,128]{3,2,1,0:T(8,128)S(1)}, f32[6,16,8,128]{3,2,1,0:T(8,128)}, u32[]{:S(2)}) copy-start(f32[6,16,8,128]{3,2,1,0:T(8,128)} %param.14) | copy-start | bytes 1179652
  6.9 0.8 %copy-start.5 = (f32[16,8,128]{2,1,0:T(8,128)S(1)}, f32[16,8,128]{2,1,0:T(8,128)}, u32[]{:S(2)}) copy-start(f32[16,8,128]{2,1,0:T(8,128)} %param.16) | copy-start | bytes 196612

commit v2 on v1

--- a/solution.py
+++ b/solution.py
@@ -52,6 +52,18 @@
     right = lax.rem(ip + 1, npass)
     left = lax.rem(ip + npass - 1, npass)
 
+    srecv[...] = jnp.zeros_like(srecv)
+
+    barrier = pltpu.get_barrier_semaphore()
+    for o in range(1, npass):
+        pl.semaphore_signal(
+            barrier, inc=1, device_id=(lax.rem(ip + o, npass), js), device_id_type=MESH
+        )
+    for o in range(1, nspan):
+        pl.semaphore_signal(
+            barrier, inc=1, device_id=(ip, lax.rem(js + o, nspan)), device_id_type=MESH
+        )
+
     loads = {}
     for n, (src, dst, name) in enumerate(
         [
@@ -65,18 +77,6 @@
     ):
         loads[name] = pltpu.make_async_copy(src, dst, in_sem.at[n])
         loads[name].start()
-
-    srecv[...] = jnp.zeros_like(srecv)
-
-    barrier = pltpu.get_barrier_semaphore()
-    for o in range(1, npass):
-        pl.semaphore_signal(
-            barrier, inc=1, device_id=(lax.rem(ip + o, npass), js), device_id_type=MESH
-        )
-    for o in range(1, nspan):
-        pl.semaphore_signal(
-            barrier, inc=1, device_id=(ip, lax.rem(js + o, nspan)), device_id_type=MESH
-        )
 
     def halo_copies(r, k):
         made = []
@@ -110,7 +110,7 @@
     halos = {(r, k): halo_copies(r, k) for r in range(2) for k in range(ITERS)}
     has_next, has_prev = js < nspan - 1, js > 0
 
-    def send_halos(r, k):
+    def pack_halos(r, k):
         for d, p in ((0, cp - 1), (1, 0)):
             for f in range(fields):
                 psend[r, k, d, pl.ds(f * cs, cs), :] = psi[r][k][
@@ -121,6 +121,8 @@
                 ssend[r, k, d, pl.ds(f * cp, cp), :] = psi[r][k][
                     pl.ds(f * plane + s, cp, stride=cs), :
                 ]
+
+    def start_halos(r, k):
         to_right, to_left, to_next, to_prev = halos[r, k]
 
         @pl.when(has_next)
@@ -205,7 +207,7 @@
     means = [mean_copies(k) for k in range(ITERS)]
     count = counts[0]
 
-    def send_face(k):
+    def pack_face(k):
         state = psi[ROTOR][k]
         tile = jnp.where(lane == fields, jnp.clip(count, 0, cp).astype(F32), 0.0)
         for f in range(fields):
@@ -215,6 +217,8 @@
                 acc = acc + w * state[pl.ds(f * plane + p * cs, cs), :]
             tile = jnp.where(lane == f, pltpu.roll(acc, f + 1, 1), tile)
         fsend[k] = tile
+
+    def start_face(k):
         for c in faces[k]:
             c.start()
 
@@ -274,9 +278,9 @@
             acc = jnp.zeros((cs, kk), F32)
             mid = jnp.zeros((cs, kk), F32)
             for g in range(fields):
-                mid = jnp.where(centre[g], -RELAX * blocks[r][0, f, g], mid)
+                mid = jnp.where(centre[g], -RELAX * blocks[r][f, 0, g], mid)
                 for b in range(1, 7):
-                    acc = jnp.where(masks[b - 1][g], blocks[r][b, f, g], acc)
+                    acc = jnp.where(masks[b - 1][g], blocks[r][f, b, g], acc)
             near.append(acc)
             main.append(mid)
         hi, lo = split(jnp.concatenate(near + main, axis=0))
@@ -339,22 +343,24 @@
                 if k + 1 < ITERS:
                     store_split(r, k + 1, p, new)
 
-        pl.loop(0, cp // 2)(pair)
-
-    pl.semaphore_wait(barrier, npass + nspan - 2)
-    loads["psi0"].wait()
-    send_halos(ROTOR, 0)
-    send_face(0)
-    loads["psi1"].wait()
-    send_halos(STATOR, 0)
+        pl.loop(0, cp // 2, unroll=cp // 2)(pair)
 
     for r in range(2):
         build_matrix(r)
-        pl.loop(0, cp)(lambda p, r=r: store_split(r, 0, p, cell(psi[r][0], p)))
+    for r in range(2):
+        loads["psi%d" % r].wait()
+        pl.loop(0, cp, unroll=cp)(lambda p, r=r: store_split(r, 0, p, cell(psi[r][0], p)))
+        pack_halos(r, 0)
+    pack_face(0)
     for r in range(2):
         loads["kap%d" % r].wait()
         coef[r][...] = RELAX / coef[r][...]
         loads["rhs%d" % r].wait()
+
+    pl.semaphore_wait(barrier, npass + nspan - 2)
+    start_face(0)
+    start_halos(ROTOR, 0)
+    start_halos(STATOR, 0)
 
     stores = []
     for k in range(ITERS):
@@ -362,8 +368,10 @@
         receive_halos(ROTOR, k)
         advance(ROTOR, k, None)
         if k + 1 < ITERS:
-            send_halos(ROTOR, k + 1)
-            send_face(k + 1)
+            pack_face(k + 1)
+            start_face(k + 1)
+            pack_halos(ROTOR, k + 1)
+            start_halos(ROTOR, k + 1)
         else:
             stores.append(pltpu.make_async_copy(psi[ROTOR][ITERS], outs[ROTOR], out_sem.at[0]))
             stores[-1].start()
@@ -371,7 +379,8 @@
         receive_halos(STATOR, k)
         advance(STATOR, k, inlet)
         if k + 1 < ITERS:
-            send_halos(STATOR, k + 1)
+            pack_halos(STATOR, k + 1)
+            start_halos(STATOR, k + 1)
     stores.append(pltpu.make_async_copy(psi[STATOR][ITERS], outs[STATOR], out_sem.at[1]))
     stores[-1].start()
     for k in range(ITERS):
@@ -436,14 +445,21 @@
     smem = pl.BlockSpec(memory_space=pltpu.SMEM)
     out = pl.pallas_call(
         functools.partial(kernel, fields, cp, cs, ca, npass, nspan),
-        out_shape=[jax.ShapeDtypeStruct((rows, ca), F32)] * 2,
+        out_shape=[pltpu.HBM((rows, ca), F32)] * 2,
         in_specs=[anywhere] * 6 + [smem] * 5,
         out_specs=[anywhere] * 2,
         scratch_shapes=scratch,
         compiler_params=pltpu.CompilerParams(
             collective_id=0, has_side_effects=True, vmem_limit_bytes=40 * 1024 * 1024
         ),
-    )(*flat, *kaps, rotor_blocks, stator_blocks, interface_block, pass_counts, tile_source)
+    )(
+        *[pltpu.with_memory_space_constraint(x, pltpu.HBM) for x in flat + kaps],
+        rotor_blocks.transpose(1, 0, 2),
+        stator_blocks.transpose(1, 0, 2),
+        interface_block,
+        pass_counts,
+        tile_source,
+    )
     return tuple(x.reshape(psi_rotor.shape) for x in out)
 
 

time: 41.4 us -> 32.4 us (0.78)
  Pallas kernels: 31.7 us -> 26.1 us
  local copies, waits for them, and re-layouts: 7.83 us -> 4.72 us
    pallas_call x1, Pallas kernels: 31.7 us -> 26.1 us  [per_device(): pl.pallas_call(functools.partial(kernel, fields, cp, cs, ca, npass, nspan...]
    unnamed x20 -> x12, local copies, waits for them, and re-layouts: 7.83 us -> 4.72 us
where the time goes in v2:
time: 32.4 us; the launch traced here: 32.1 us
  Pallas kernels  26.1 us (81%)
  local copies, waits for them, and re-layouts  4.72 us (15%)
  between operations  1.32 us (4%)
    pallas_call x1, Pallas kernels, per_device(): pl.pallas_call(functools.partial(kernel, fields, cp, cs, ca, npass, nspan...  26.1 us
    unnamed x12, local copies, waits for them, and re-layouts  4.72 us

profile of v2, /device:TPU:0, one launch (start us, length us, event | category | flops | bytes accessed | tf_op | source)
XLA Modules:
  0.0 32.1 jit_solution(10441656070957988915)
XLA Ops:
  1.3 0.0 copy-start.2
  1.3 0.0 copy-start.3
  1.3 0.7 %copy-done.2 = f32[6,6]{1,0:T(8,128)S(1)} copy-done((f32[6,6]{1,0:T(8,128)S(1)}, f32[6,6]{1,0:T(8,128)}, u32[]{:S(2)}) %copy-start.2) | copy-done | bytes 168
  2.0 0.0 copy-done.3
  2.0 0.0 copy-start
  2.0 0.7 %copy-done = f32[7,6,6]{2,0,1:T(8,128)S(1)} copy-done((f32[7,6,6]{2,0,1:T(8,128)S(1)}, f32[7,6,6]{2,0,1:T(8,128)}, u32[]{:S(2)}) %copy-start) | copy-done | bytes 1032
  2.7 0.0 copy-start.1
  2.7 0.7 %copy-done.1 = f32[7,6,6]{2,0,1:T(8,128)S(1)} copy-done((f32[7,6,6]{2,0,1:T(8,128)S(1)}, f32[7,6,6]{2,0,1:T(8,128)}, u32[]{:S(2)}) %copy-start.1) | copy-done | bytes 1032
  3.4 26.1 %shard_map.122 = (f32[768,128]{1,0:T(8,128)}, f32[768,128]{1,0:T(8,128)}) custom-call(f32[768,128]{1,0:T(8,128)} %bitcast.14, f32[768,128]{1,0:T(8,128)} %bitcast.15, f32[768,128]{1,0:T(8,128)} %bitcast.16, f32[768,128]{1,0:T(8,128)} %bitcast.17, f32[128,128]{1,0:T(8,128)} %bitcast.18, f32[128,128]{1,0:T(8,128)} %bitcast.19, f32[6,7,6]{2,1,0:T(8,128)S(1)} %bitcast.10, ...), custom_call_target="tpu_custom_call" | custom-call | tf_op jit(solution)/shard_map/pallas_call | solution.py:446
  29.5 0.0 copy-start.4
  29.5 1.8 %copy.16 = f32[6,16,8,128]{3,2,1,0:T(8,128)} copy(f32[6,16,8,128]{3,2,1,0:T(8,128)} %bitcast.13) | data formatting | bytes 786432
  31.4 0.0 copy-done.4
  31.4 0.7 %copy.17 = f32[6,16,8,128]{3,2,1,0:T(8,128)} copy(f32[6,16,8,128]{3,2,1,0:T(8,128)S(1)} %bitcast.12) | data formatting | bytes 786432
Async XLA Ops:
  1.3 0.7 %copy-start.2 = (f32[6,6]{1,0:T(8,128)S(1)}, f32[6,6]{1,0:T(8,128)}, u32[]{:S(2)}) copy-start(f32[6,6]{1,0:T(8,128)} %refs_8_.1) | copy-start | bytes 436
  1.3 0.7 %copy-start.3 = (s32[8]{0:T(128)S(1)}, s32[8]{0:T(128)}, u32[]{:S(2)}) copy-start(s32[8]{0:T(128)} %refs_10_.1) | copy-start | bytes 100
  2.0 0.7 %copy-start = (f32[7,6,6]{2,0,1:T(8,128)S(1)}, f32[7,6,6]{2,0,1:T(8,128)}, u32[]{:S(2)}) copy-start(f32[7,6,6]{2,0,1:T(8,128)} %param.17) | copy-start | bytes 3028
  2.7 0.7 %copy-start.1 = (f32[7,6,6]{2,0,1:T(8,128)S(1)}, f32[7,6,6]{2,0,1:T(8,128)}, u32[]{:S(2)}) copy-start(f32[7,6,6]{2,0,1:T(8,128)} %param.18) | copy-start | bytes 3028
  29.5 1.8 %copy-start.4 = (f32[768,128]{1,0:T(8,128)S(1)}, f32[768,128]{1,0:T(8,128)}, u32[]{:S(2)}) copy-start(f32[768,128]{1,0:T(8,128)} %get-tuple-element.5) | copy-start | bytes 1179652
